TPU v7x, 32 devices: a whole 2x2x4 slice. The times are simulated.
32 devices in a mesh: group: 2 (over y), fin: 4 (over z), fout: 2 (over x), rep: 2 (over core).
Axes of the slice: x: 2, y: 2, z: 4, core: 2. Of those that a mesh axis runs over, the one named last changes fastest.
Arguments:
- tokens: bfloat16 [1024, 8192], P(('group', 'rep'), 'fin'), parts along dimension 0, may hold values from -6 to 6
- weight_blocks: bfloat16 [4, 2, 448, 128, 128], P('fin', 'fout'), may hold values from -0.125 to 0.125
- block_index: int32 [4, 2, 448, 2], P('fin', 'fout'), may hold values from 0 to 55, as said below
- block_count: int32 [4, 2], P('fin', 'fout'), may hold values from 112 to 448, as said below
- cotangent: bfloat16 [1024, 14336], P(('group', 'rep', 'fin'), 'fout'), parts along dimension 0, may hold values from -6 to 6
Outputs:
- activated: bfloat16 [1024, 14336], P(('group', 'rep', 'fin'), 'fout'), parts along dimension 0
- input_grad: float32 [1024, 8192], P(('group', 'rep'), ('fin', 'fout')), parts along dimension 0
- weight_grad: float32 [8, 2, 448, 128, 128], P(('group', 'fin'), 'fout', 'rep'), parts along dimension 0
There are 2 independent parts, one for each index of `group`. A program takes and returns all parts, laid end to end along the dimension named above; an argument that names none is the same for every part. Nothing has to cross between parts.
Inputs may be any that keep to these rules, and one draw needn't show every extreme that they name: `block_index`: within a shard the 448 slots name distinct blocks of the shard's 16 x 56 grid as (row block, column block); only the first block_count slots are listed. `block_count`: some shard lists all 448 slots.
All inputs are finite; a program needn't handle non-finite values.
Results may differ from a plain program's by a relative error of at most 0.0027.
Values may be sent and summed in bfloat16 or wider, within the bound.
A program may use at most 320 MiB of HBM per device.

v0:
```python
import jax
import jax.numpy as jnp
from jax import lax
from jax.sharding import PartitionSpec as P

BLK = 128


def gelu_value(v):
    return v * (0.5 + 0.5 * lax.erf(v * 0.7071067811865476))


def gelu_slope(v):
    cdf = 0.5 + 0.5 * lax.erf(v * 0.7071067811865476)
    return cdf + v * jnp.exp(-0.5 * v * v) * 0.3989422804014327


def local(tokens, weight_blocks, block_index, block_count, cotangent):
    blocks = weight_blocks[0, 0]
    index = block_index[0, 0]
    count = block_count[0, 0]
    slots = blocks.shape[0]
    rows_total, width_in = tokens.shape
    own_rows, width_out = cotangent.shape
    row_blocks = width_in // BLK
    col_blocks = width_out // BLK
    live = jnp.arange(slots, dtype=jnp.int32) < count
    live_full = live.astype(jnp.float32)
    row_ids = index[:, 0]
    col_ids = index[:, 1]
    masked = blocks * live.astype(jnp.bfloat16)[:, None, None]
    rows_low = (row_ids[:, None] == jnp.arange(row_blocks, dtype=jnp.int32)[None, :]).astype(
        jnp.bfloat16
    )
    cols_low = (col_ids[:, None] == jnp.arange(col_blocks, dtype=jnp.int32)[None, :]).astype(
        jnp.bfloat16
    )
    dense = jnp.einsum(
        "gr,gc,gij->ricj", rows_low, cols_low, masked, preferred_element_type=jnp.float32
    )
    dense = dense.astype(jnp.bfloat16).reshape(width_in, width_out)
    pre = lax.psum_scatter(
        jnp.dot(tokens, dense, preferred_element_type=jnp.float32),
        "fin",
        scatter_dimension=0,
        tiled=True,
    )
    activated = gelu_value(pre).astype(jnp.bfloat16)
    saved = pre.astype(jnp.bfloat16)
    slope = gelu_slope(lax.optimization_barrier(saved).astype(jnp.float32))
    grad_rows = (cotangent.astype(jnp.float32) * slope).astype(jnp.bfloat16)
    grad_all = lax.all_gather(grad_rows, "fin", axis=0, tiled=True)
    input_part = lax.dot_general(
        grad_all, dense, (((1,), (1,)), ((), ())), preferred_element_type=jnp.float32
    )
    dense_grad = lax.dot_general(
        tokens, grad_all, (((0,), (0,)), ((), ())), preferred_element_type=jnp.float32
    )
    dense_grad = dense_grad.reshape(row_blocks, BLK, col_blocks, BLK)
    slot_grad = dense_grad[row_ids, :, col_ids, :]
    slot_grad = slot_grad * live_full[:, None, None]
    input_grad = lax.psum_scatter(input_part, "fout", scatter_dimension=1, tiled=True)
    weight_grad = lax.psum_scatter(slot_grad, "rep", scatter_dimension=0, tiled=True)
    return (activated, input_grad, weight_grad.reshape(1, 1, weight_grad.shape[0], BLK, BLK))


def solution(mesh):
    return jax.shard_map(
        local,
        mesh=mesh,
        in_specs=(
            P(("group", "rep"), "fin"),
            P("fin", "fout", None, None, None),
            P("fin", "fout", None, None),
            P("fin", "fout"),
            P(("group", "rep", "fin"), "fout"),
        ),
        out_specs=(
            P(("group", "rep", "fin"), "fout"),
            P(("group", "rep"), ("fin", "fout")),
            P(("group", "fin"), "fout", "rep", None, None),
        ),
        check_vma=False,
    )
```

profile of v0, /device:TPU:0, one launch (start us, length us, event | category | flops | bytes accessed | tf_op | source)
XLA Modules:
  0.0 565.2 jit_solution(797296928811746115)
XLA Ops:
  7.2 0.0 reduce-scatter.10.cloned.1.call-start
  8.0 0.6 fusion.30
  8.5 1.4 fusion.27
  9.9 13.7 %bitcast_multiply_fusion = bf16[448,128,128]{2,1,0:T(8,128)(2,1)} fusion(bf16[1,1,448,128,128]{4,3,2,1,0:T(8,128)(2,1)} %param.6, bf16[448]{0:T(512)(128)(2,1)S(1)} %get-tuple-element.18), kind=kLoop, calls=%fused_computation.10 | loop fusion | flops 7340032 | bytes 29361024 | tf_op jit(solution)/shard_map/mul | solution.py:31
  23.7 50.1 %convert_bitcast_fusion = bf16[16,128,56,128]{3,0,1,2:T(8,128)(2,1)} fusion(bf16[448,128,128]{2,1,0:T(8,128)(2,1)} %bitcast_multiply_fusion, f32[448,16]{0,1:T(8,128)S(1)} %fusion.24, f32[448,56]{0,1:T(8,128)S(1)} %fusion.23), kind=kOutput, calls=%fused_computation.5 | convolution fusion | flops 13168418816 | bytes 44169216 | tf_op jit(solution)/shard_map/gr,gc,gij->ricj/dot_general | solution.py:38
  73.8 26.0 %copy.23 = bf16[16,128,56,128]{3,2,1,0:T(8,128)(2,1)} copy(bf16[16,128,56,128]{3,0,1,2:T(8,128)(2,1)} %convert_bitcast_fusion) | data formatting | bytes 58720256 | tf_op jit(solution)/shard_map/convert_element_type | solution.py:41
  99.8 20.1 %fusion.8 = f32[256,7168]{0,1:T(8,128)} fusion(bf16[256,2048]{1,0:T(8,128)(2,1)S(1)} %copy-done, bf16[256,8,56,128]{3,2,1,0:T(8,128)(2,1)} %bitcast.43), kind=kOutput, calls=%fused_computation.13 | convolution fusion | flops 7516192768 | bytes 37748736 | tf_op jit(solution)/shard_map/dot_general | solution.py:43
  119.9 8.4 %copy.29 = f32[256,7168]{1,0:T(8,128)} copy(f32[256,7168]{0,1:T(8,128)} %fusion.8) | data formatting | bytes 14680064
  128.3 0.0 reduce-scatter.10.cloned.1.call-update
  128.4 0.0 all-gather.2.cloned.1.call-start
  128.4 130.5 %reduce-scatter.10.cloned.1.call-done = f32[64,7168]{1,0:T(8,128)} async-done(((f32[256,7168]{1,0:T(8,128)}), f32[64,7168]{1,0:T(8,128)}) %reduce-scatter.10.cloned.1.call-update) | async-done | bytes 1835024 | tf_op jit(solution)/shard_map/reduce_scatter | solution.py:42
  258.9 3.4 fusion.32
  262.3 1.8 fusion.20
  264.1 0.0 reduce-scatter.6.cloned.1.call-start
  264.2 72.7 %all-gather.2.cloned.1.call-done = bf16[256,7168]{1,0:T(8,128)(2,1)} async-done(((bf16[64,7168]{1,0:T(8,128)(2,1)}), bf16[256,7168]{1,0:T(8,128)(2,1)}) %all-gather.2.cloned.1.call-update) | async-done | bytes 3670032 | tf_op jit(solution)/shard_map/all_gather | solution.py:52
  336.9 15.6 %fusion = f32[256,2048]{1,0:T(8,128)} fusion(bf16[256,7168]{1,0:T(8,128)(2,1)} %all-gather.2.cloned.1.call-done, bf16[256,8,56,128]{3,2,1,0:T(8,128)(2,1)} %bitcast.44), kind=kOutput, calls=%fused_computation.1 | convolution fusion | flops 7516192768 | bytes 35127296 | tf_op jit(solution)/shard_map/dot_general | solution.py:53
  352.5 0.0 reduce-scatter.8.cloned.1.call-start
  352.6 23.0 %convolution_bitcast_fusion = f32[896,8,16,128]{3,1,2,0:T(8,128)} fusion(bf16[256,7168]{1,0:T(8,128)(2,1)} %all-gather.2.cloned.1.call-done, bf16[256,2048]{1,0:T(8,128)(2,1)S(1)} %copy-done), kind=kOutput, calls=%fused_computation.8 | convolution fusion | flops 7516192768 | bytes 63438848 | tf_op jit(solution)/shard_map/dot_general | solution.py:56
  375.5 39.5 %copy.32 = f32[896,8,16,128]{3,2,1,0:T(8,128)} copy(f32[896,8,16,128]{3,1,2,0:T(8,128)} %convolution_bitcast_fusion) | data formatting | bytes 117440512
  415.1 53.6 %copy.27 = f32[16,128,56,128]{3,1,2,0:T(8,128)} copy(f32[16,128,56,128]{1,0,3,2:T(8,128)} %bitcast.42) | data formatting | bytes 117440512 | tf_op jit(solution)/shard_map/reshape | solution.py:59
  468.7 28.9 %gather_fusion = f32[448,128,128]{2,1,0:T(8,128)} fusion(f32[16,128,56,128]{3,1,2,0:T(8,128)} %copy.27, s32[448]{0:T(512)S(1)} %bitcast.45), kind=kCustom, calls=%fused_computation | custom fusion | bytes 58723840 | tf_op jit(solution)/shard_map/gather | solution.py:60
  497.6 21.7 %broadcast_multiply_fusion = f32[448,128,128]{2,1,0:T(8,128)} fusion(f32[448,128,128]{2,1,0:T(8,128)} %gather_fusion, f32[448]{0:T(512)S(1)} %copy-done.4), kind=kLoop, calls=%fused_computation.12 | loop fusion | flops 7340032 | bytes 58722048 | tf_op jit(solution)/shard_map/mul | solution.py:61
  519.3 0.0 reduce-scatter.6.cloned.1.call-done
  519.4 39.3 %reduce-scatter.8.cloned.1.call-done = f32[224,128,128]{2,1,0:T(8,128)} async-done(((f32[448,128,128]{2,1,0:T(8,128)}), f32[224,128,128]{2,1,0:T(8,128)}) %reduce-scatter.8.cloned.1.call-update) | async-done | bytes 14680080 | tf_op jit(solution)/shard_map/reduce_scatter | solution.py:63
  (15 shorter events, 0.1 us)
Async XLA Ops:
  7.2 92.7 %copy-start = (bf16[256,2048]{1,0:T(8,128)(2,1)S(1)}, bf16[256,2048]{1,0:T(8,128)(2,1)}, u32[]{:S(2)}) copy-start(bf16[256,2048]{1,0:T(8,128)(2,1)} %param.5) | copy-start | bytes 3145732
  7.2 251.8 %reduce-scatter.10.cloned.1.call-start = ((), (), s32[]{:S(2)}) async-start(), calls=%async_computation.6 | async-start | bytes 9175040 | tf_op jit(solution)/shard_map/reduce_scatter | solution.py:42
  128.3 134.0 %copy-start.3 = (bf16[64,7168]{1,0:T(8,128)(2,1)S(1)}, bf16[64,7168]{1,0:T(8,128)(2,1)}, u32[]{:S(2)}) copy-start(bf16[64,7168]{1,0:T(8,128)(2,1)} %param.9) | copy-start | bytes 2752516
  128.4 208.5 %all-gather.2.cloned.1.call-start = ((), (), s32[]{:S(2)}) async-start(), calls=%async_computation.3 | async-start | bytes 4587520 | tf_op jit(solution)/shard_map/all_gather | solution.py:52
  264.1 255.2 %reduce-scatter.6.cloned.1.call-start = ((), (), s32[]{:S(2)}) async-start(), calls=%async_computation.4 | async-start | bytes 3145728 | tf_op jit(solution)/shard_map/reduce_scatter | solution.py:62
  352.5 206.1 %reduce-scatter.8.cloned.1.call-start = ((), (), s32[]{:S(2)}) async-start(), calls=%async_computation.5 | async-start | bytes 44040192 | tf_op jit(solution)/shard_map/reduce_scatter | solution.py:63
  415.1 53.6 %copy-start.2 = (s32[448,1]{0,1:T(1,128)S(1)}, s32[448,1]{0,1:T(1,128)}, u32[]{:S(2)}) copy-start(s32[448,1]{0,1:T(1,128)} %get-tuple-element.14) | copy-start | bytes 5380
  468.7 28.9 %copy-start.4 = (f32[448]{0:T(512)S(1)}, f32[448]{0:T(512)}, u32[]{:S(2)}) copy-start(f32[448]{0:T(512)} %get-tuple-element.17) | copy-start | bytes 5380
  519.3 39.3 %copy-start.1 = (bf16[256,2048]{1,0:T(8,128)(2,1)S(1)}, bf16[256,2048]{1,0:T(8,128)(2,1)}, u32[]{:S(2)}) copy-start(bf16[256,2048]{1,0:T(8,128)(2,1)} %param.5) | copy-start | bytes 3145732
Sparse Core Ops, SparseCore 0:
  128.5 130.4 reduce-scatter.9
  264.2 72.6 all-gather.1
  352.6 30.4 reduce-scatter.5
  519.4 39.1 reduce-scatter.7
where the time goes:
time: 566 us; the launch traced here: 565 us
  waiting for transfers between devices  243 us (43%)
  local copies, waits for them, and re-layouts  156 us (28%)
  matrix products  109 us (19%)
  other arithmetic  42.6 us (8%)
  between operations  14.5 us (3%)
    reduce_scatter x1, waiting for transfers between devices, local(): lax.psum_scatter(jnp.dot(tokens, dense, preferred_element_type=jnp.float3...  131 us
    all_gather x1, waiting for transfers between devices, local(): grad_all = lax.all_gather(grad_rows, 'fin', axis=0, tiled=True)  72.7 us
    reshape x1, local copies, waits for them, and re-layouts, local(): dense_grad = dense_grad.reshape(row_blocks, BLK, col_blocks, BLK)  53.6 us
    dot_general x1, matrix products, local(): jnp.einsum('gr,gc,gij->ricj', rows_low, cols_low, masked, preferred_eleme...  50.1 us
    unnamed x12, local copies, waits for them, and re-layouts  47.9 us
    reduce_scatter x1, waiting for transfers between devices, local(): lax.psum_scatter(slot_grad, 'rep', scatter_dimension=0, tiled=True)  39.3 us
    gather x1, local copies, waits for them, and re-layouts, local(): slot_grad = dense_grad[row_ids, :, col_ids, :]  28.9 us
    convert_element_type x1, local copies, waits for them, and re-layouts, local(): dense = dense.astype(jnp.bfloat16).reshape(width_in, width_out)  26 us
  transfers between devices with their start and end apart: 4, of which 3 were waited for; matrix products, arithmetic and copies ran while one was open for 29% of the time, Pallas kernels for 0%

commit v1 on v0

v1 whole, which is shorter than its diff:
```python
import functools

import jax
import jax.numpy as jnp
from jax import lax
from jax.experimental import pallas as pl
from jax.experimental.pallas import tpu as pltpu
from jax.sharding import PartitionSpec as P

BLK = 128


def gelu_value(v):
    return v * (0.5 + 0.5 * lax.erf(v * 0.7071067811865476))


def gelu_slope(v):
    cdf = 0.5 + 0.5 * lax.erf(v * 0.7071067811865476)
    return cdf + v * jnp.exp(-0.5 * v * v) * 0.3989422804014327


def divisor(n, most):
    d = most
    while n % d:
        d -= 1
    return d


def fill_dense(step, rows, cols, count, blocks, dense):
    group = blocks.shape[0]

    @pl.when(step == 0)
    def _():
        def clear(i, carry):
            dense[pl.ds(pl.multiple_of(i * BLK, BLK), BLK), :] = jnp.zeros(
                (BLK, dense.shape[1]), dense.dtype
            )
            return carry

        lax.fori_loop(0, dense.shape[0] // BLK, clear, 0)

    for j in range(group):
        slot = step * group + j

        @pl.when(slot < count[0])
        def _():
            r = pl.multiple_of(rows[slot] * BLK, BLK)
            c = pl.multiple_of(cols[slot] * BLK, BLK)
            dense[pl.ds(r, BLK), pl.ds(c, BLK)] = blocks[j]


def forward_kernel(fills, chunk, rows, cols, count, blocks, tokens, out, dense):
    step = pl.program_id(0)

    @pl.when(step < fills)
    def _():
        fill_dense(step, rows, cols, count, blocks, dense)

    @pl.when(step >= fills)
    def _():
        c = pl.multiple_of((step - fills) * chunk, chunk)
        out[...] = jnp.dot(
            tokens[...], dense[:, pl.ds(c, chunk)], preferred_element_type=jnp.float32
        )


def backward_kernel(fills, chunk, rows, cols, count, blocks, grads, out, dense):
    step = pl.program_id(0)

    @pl.when(step < fills)
    def _():
        fill_dense(step, rows, cols, count, blocks, dense)

    @pl.when(step >= fills)
    def _():
        r = pl.multiple_of((step - fills) * chunk, chunk)
        out[...] = lax.dot_general(
            grads[...],
            dense[pl.ds(r, chunk), :],
            (((1,), (1,)), ((), ())),
            preferred_element_type=jnp.float32,
        )


def dense_product(kernel, rows, cols, count, blocks, left, width_in, width_out, chunk, out_width):
    slots = blocks.shape[0]
    group = divisor(slots, 28)
    fills = slots // group
    steps = out_width // chunk
    height = left.shape[0]
    return pl.pallas_call(
        functools.partial(kernel, fills, chunk),
        out_shape=jax.ShapeDtypeStruct((height, out_width), jnp.float32),
        grid_spec=pltpu.PrefetchScalarGridSpec(
            num_scalar_prefetch=3,
            grid=(fills + steps,),
            in_specs=[
                pl.BlockSpec((group, BLK, BLK), lambda i, *_: (jnp.minimum(i, fills - 1), 0, 0)),
                pl.BlockSpec(left.shape, lambda i, *_: (0, 0)),
            ],
            out_specs=pl.BlockSpec((height, chunk), lambda i, *_: (0, jnp.maximum(i - fills, 0))),
            scratch_shapes=[pltpu.VMEM((width_in, width_out), jnp.bfloat16)],
        ),
        compiler_params=pltpu.CompilerParams(
            dimension_semantics=("arbitrary",), vmem_limit_bytes=60 * 1024 * 1024
        ),
        cost_estimate=pl.CostEstimate(
            flops=2 * height * width_in * width_out,
            bytes_accessed=2 * blocks.size + 4 * height * out_width,
            transcendentals=0,
        ),
    )(rows, cols, count, blocks, left)


def slot_kernel(group, rows, cols, count, turned, grads, out):
    step = pl.program_id(0)
    for j in range(group):
        slot = step * group + j
        live = slot < count[0]

        @pl.when(live)
        def _():
            r = pl.multiple_of(rows[slot] * BLK, BLK)
            c = pl.multiple_of(cols[slot] * BLK, BLK)
            out[j] = jnp.dot(
                turned[pl.ds(r, BLK), :],
                grads[:, pl.ds(c, BLK)],
                preferred_element_type=jnp.float32,
            )

        @pl.when(jnp.logical_not(live))
        def _():
            out[j] = jnp.zeros((BLK, BLK), jnp.float32)


def slot_products(rows, cols, count, turned, grads):
    slots = rows.shape[0]
    group = divisor(slots, 14)
    return pl.pallas_call(
        functools.partial(slot_kernel, group),
        out_shape=jax.ShapeDtypeStruct((slots, BLK, BLK), jnp.float32),
        grid_spec=pltpu.PrefetchScalarGridSpec(
            num_scalar_prefetch=3,
            grid=(slots // group,),
            in_specs=[
                pl.BlockSpec(turned.shape, lambda i, *_: (0, 0)),
                pl.BlockSpec(grads.shape, lambda i, *_: (0, 0)),
            ],
            out_specs=pl.BlockSpec((group, BLK, BLK), lambda i, *_: (i, 0, 0)),
        ),
        compiler_params=pltpu.CompilerParams(
            dimension_semantics=("arbitrary",), vmem_limit_bytes=56 * 1024 * 1024
        ),
        cost_estimate=pl.CostEstimate(
            flops=2 * slots * BLK * BLK * grads.shape[0],
            bytes_accessed=4 * slots * BLK * BLK + 2 * grads.size,
            transcendentals=0,
        ),
    )(rows, cols, count, turned, grads)


def local(tokens, weight_blocks, block_index, block_count, cotangent):
    blocks = weight_blocks[0, 0]
    rows = block_index[0, 0, :, 0]
    cols = block_index[0, 0, :, 1]
    count = block_count[0]
    slots = blocks.shape[0]
    width_in = tokens.shape[1]
    width_out = cotangent.shape[1]
    turned = lax.all_gather(tokens, "rep", axis=0, tiled=True).T
    part = dense_product(
        forward_kernel, rows, cols, count, blocks, tokens, width_in, width_out, 512, width_out
    )
    pre = lax.psum_scatter(part, "fin", scatter_dimension=0, tiled=True)
    activated = gelu_value(pre).astype(jnp.bfloat16)
    saved = pre.astype(jnp.bfloat16)
    slope = gelu_slope(lax.optimization_barrier(saved).astype(jnp.float32))
    grad_rows = (cotangent.astype(jnp.float32) * slope).astype(jnp.bfloat16)
    grads = lax.all_gather(grad_rows, "fin", axis=0, tiled=True)
    both = lax.all_gather(grads, "rep", axis=0, tiled=True)
    input_part = dense_product(
        backward_kernel, rows, cols, count, blocks, grads, width_in, width_out, 256, width_in
    )
    input_grad = lax.psum_scatter(input_part, "fout", scatter_dimension=1, tiled=True)
    half = slots // lax.axis_size("rep")
    first = lax.axis_index("rep") * half
    weight_grad = slot_products(
        lax.dynamic_slice_in_dim(rows, first, half),
        lax.dynamic_slice_in_dim(cols, first, half),
        count - first,
        turned,
        both,
    )
    return (activated, input_grad, weight_grad.reshape(1, 1, half, BLK, BLK))


def solution(mesh):
    return jax.shard_map(
        local,
        mesh=mesh,
        in_specs=(
            P(("group", "rep"), "fin"),
            P("fin", "fout", None, None, None),
            P("fin", "fout", None, None),
            P("fin", "fout"),
            P(("group", "rep", "fin"), "fout"),
        ),
        out_specs=(
            P(("group", "rep", "fin"), "fout"),
            P(("group", "rep"), ("fin", "fout")),
            P(("group", "fin"), "fout", "rep", None, None),
        ),
        check_vma=False,
    )
```

time: 566 us -> 335 us (0.59)
  local copies, waits for them, and re-layouts: 156 us -> 3.98 us
  matrix products: 109 us -> 0 us
  Pallas kernels: 0 us -> 105 us
  other arithmetic: 42.6 us -> 5.19 us
  waiting for transfers between devices: 243 us -> 206 us
    dot_general x4 -> x0, matrix products: 109 us -> none  [the longest x1 50.1 us: local(): jnp.einsum('gr,gc,gij->ricj', rows_low, cols_low, masked, preferred_eleme...]
    pallas_call x0 -> x3, Pallas kernels: none -> 105 us  [the longest x2 53.4 us: dense_product(): pl.pallas_call(functools.partial(kernel, fills, chunk), out_shape=jax.Sha...]
    reshape x1 -> x0, local copies, waits for them, and re-layouts: 53.6 us -> none  [local(): dense_grad = dense_grad.reshape(row_blocks, BLK, col_blocks, BLK)]
    unnamed x12 -> x9, local copies, waits for them, and re-layouts: 47.9 us -> 1.97 us
    reduce_scatter x2 -> x1, waiting for transfers between devices: 170 us -> 131 us  [local(): pre = lax.psum_scatter(part, 'fin', scatter_dimension=0, tiled=True)]
    mul x2 -> x0, other arithmetic: 35.4 us -> none  [the longest x1 21.7 us: local(): slot_grad = slot_grad * live_full[:, None, None]]
    gather x1 -> x0, local copies, waits for them, and re-layouts: 28.9 us -> none  [local(): slot_grad = dense_grad[row_ids, :, col_ids, :]]
    convert_element_type x1 -> x0, local copies, waits for them, and re-layouts: 26 us -> none  [local(): dense = dense.astype(jnp.bfloat16).reshape(width_in, width_out)]
  transfers between devices with their start and end apart: 4 -> 5, of which waited for: 3 -> 3; matrix products, arithmetic and copies ran while one was open for 29% -> 1% of each run, Pallas kernels for 0% -> 23%
where the time goes in v1:
time: 335 us
  waiting for transfers between devices  206 us (61%)
  Pallas kernels  105 us (31%)
  between operations  14.5 us (4%)
  other arithmetic  5.19 us (2%)
  local copies, waits for them, and re-layouts  3.98 us (1%)
    reduce_scatter x1, waiting for transfers between devices, local(): pre = lax.psum_scatter(part, 'fin', scatter_dimension=0, tiled=True)  131 us
    all_gather x1, waiting for transfers between devices, local(): grads = lax.all_gather(grad_rows, 'fin', axis=0, tiled=True)  71.3 us
    pallas_call x2, Pallas kernels, dense_product(): pl.pallas_call(functools.partial(kernel, fills, chunk), out_shape=jax.Sha...  53.4 us
    pallas_call x1, Pallas kernels, slot_products(): pl.pallas_call(functools.partial(slot_kernel, group), out_shape=jax.Shape...  51.7 us
  transfers between devices with their start and end apart: 5, of which 3 were waited for; matrix products, arithmetic and copies ran while one was open for 1% of the time, Pallas kernels for 23%

profile of v1, /device:TPU:0, one launch (start us, length us, event | category | flops | bytes accessed | tf_op | source)
XLA Modules:
  0.0 334.9 jit_solution(1642743684176116479)
XLA Ops:
  7.2 0.0 reduce-scatter.3.cloned.1.call-start
  7.9 1.4 fusion.9
  9.2 26.8 %shard_map.76 = f32[256,7168]{1,0:T(8,128)} custom-call(s32[448]{0:T(512)} %bitcast.16, s32[448]{0:T(512)} %bitcast.14, s32[1]{0:T(128)} %bitcast.9.count, bf16[448,128,128]{2,1,0:T(8,128)(2,1)} %bitcast.20, bf16[256,2048]{1,0:T(8,128)(2,1)} %tokens.1), custom_call_target="tpu_custom_call" | custom-call | flops 7516192768 | bytes 22020096 | tf_op jit(solution)/shard_map/pallas_call | solution.py:91
  36.0 0.0 reduce-scatter.3.cloned.1.call-update
  36.0 0.0 copy-start.1
  36.0 0.0 all-gather.4.cloned.1.call-start
  36.1 130.6 %reduce-scatter.3.cloned.1.call-done = f32[64,7168]{1,0:T(8,128)} async-done(((f32[256,7168]{1,0:T(8,128)}), f32[64,7168]{1,0:T(8,128)}) %reduce-scatter.3.cloned.1.call-update) | async-done | bytes 1835024 | tf_op jit(solution)/shard_map/reduce_scatter | solution.py:174
  166.7 3.4 %fusion.8 = (bf16[64,7168]{1,0:T(8,128)(2,1)S(1)}, bf16[64,7168]{1,0:T(8,128)(2,1)}) fusion(f32[64,7168]{1,0:T(8,128)} %reduce-scatter.3.cloned.1.call-done), kind=kLoop, calls=%fused_computation.15 | loop fusion | flops 2752512 | bytes 3670016 | tf_op jit(solution)/shard_map/convert_element_type | solution.py:176
  170.1 1.8 fusion.7
  171.9 0.0 all-gather.4.cloned.1.call-update
  171.9 0.0 all-gather.6.cloned.1.call-start
  171.9 1.3 copy.8
  173.2 0.0 all-gather.6.cloned.1.call-update
  173.3 0.0 all-gather.8.cloned.1.call-start
  173.3 71.3 %all-gather.4.cloned.1.call-done.grads = bf16[256,7168]{1,0:T(8,128)(2,1)} async-done(((bf16[64,7168]{1,0:T(8,128)(2,1)}), bf16[256,7168]{1,0:T(8,128)(2,1)}) %all-gather.4.cloned.1.call-update) | async-done | bytes 3670032 | tf_op jit(solution)/shard_map/all_gather | solution.py:179
  244.7 0.0 all-gather.8.cloned.1.call-update
  244.7 0.0 reduce-scatter.5.cloned.1.call-start
  244.7 26.6 %shard_map.77 = f32[256,2048]{1,0:T(8,128)} custom-call(s32[448]{0:T(512)} %bitcast.17, s32[448]{0:T(512)} %bitcast.15, s32[1]{0:T(128)} %bitcast.10.count, bf16[448,128,128]{2,1,0:T(8,128)(2,1)} %bitcast.21, bf16[256,7168]{1,0:T(8,128)(2,1)} %all-gather.4.cloned.1.call-done.grads), custom_call_target="tpu_custom_call" | custom-call | flops 7516192768 | bytes 16777216 | tf_op jit(solution)/shard_map/pallas_call | solution.py:91
  271.3 0.0 reduce-scatter.5.cloned.1.call-update
  271.4 0.6 copy-done.2
  272.0 0.1 copy-done.3
  272.0 0.7 constant_dynamic-slice_fusion
  272.7 4.0 %all-gather.8.cloned.1.call-done.grads = bf16[512,7168]{1,0:T(8,128)(2,1)} async-done(((bf16[256,7168]{1,0:T(8,128)(2,1)}), bf16[512,7168]{1,0:T(8,128)(2,1)}) %all-gather.8.cloned.1.call-update) | async-done | bytes 7340048 | tf_op jit(solution)/shard_map/all_gather | solution.py:180
  276.7 51.7 %shard_map.78 = f32[224,128,128]{2,1,0:T(8,128)} custom-call(s32[224]{0:T(256)} %bitcast.19, s32[224]{0:T(256)} %bitcast.18, s32[1]{0:T(128)S(6)} %sub.7.count, bf16[2048,512]{1,0:T(8,128)(2,1)} %bitcast.13, bf16[512,7168]{1,0:T(8,128)(2,1)} %all-gather.8.cloned.1.call-done.grads), custom_call_target="tpu_custom_call" | custom-call | flops 3758096384 | bytes 22020096 | tf_op jit(solution)/shard_map/pallas_call | solution.py:139
  (7 shorter events, 0.0 us)
Async XLA Ops:
  7.2 159.5 %reduce-scatter.3.cloned.1.call-start = ((), (), s32[]{:S(2)}) async-start(), calls=%async_computation.2 | async-start | bytes 9175040 | tf_op jit(solution)/shard_map/reduce_scatter | solution.py:174
  36.0 134.0 %copy-start.1 = (bf16[64,7168]{1,0:T(8,128)(2,1)S(1)}, bf16[64,7168]{1,0:T(8,128)(2,1)}, u32[]{:S(2)}) copy-start(bf16[64,7168]{1,0:T(8,128)(2,1)} %param.9) | copy-start | bytes 2752516
  36.0 208.6 %all-gather.4.cloned.1.call-start = ((), (), s32[]{:S(2)}) async-start(), calls=%async_computation.3 | async-start | bytes 4587520 | tf_op jit(solution)/shard_map/all_gather | solution.py:179
  170.1 1.9 copy-start
  171.9 100.8 %all-gather.6.cloned.1.call-start = ((), (), s32[]{:S(2)}) async-start(), calls=%async_computation.5 | async-start | bytes 3145728 | tf_op jit(solution)/shard_map/all_gather | solution.py:170
  173.3 103.4 %all-gather.8.cloned.1.call-start = ((), (), s32[]{:S(2)}) async-start(), calls=%async_computation.6 | async-start | bytes 11010048 | tf_op jit(solution)/shard_map/all_gather | solution.py:180
  244.7 83.7 %reduce-scatter.5.cloned.1.call-start = ((), (), s32[]{:S(2)}) async-start(), calls=%async_computation.4 | async-start | bytes 3145728 | tf_op jit(solution)/shard_map/reduce_scatter | solution.py:184
  271.3 0.6 copy-start.2
  271.3 0.7 copy-start.3
Sparse Core Ops, SparseCore 0:
  36.1 130.4 reduce-scatter.2
  172.0 72.6 all-gather.3
  246.8 8.9 all-gather.5
  257.1 19.4 all-gather.7
  279.3 33.0 reduce-scatter.4
